TPU v7x, 32 devices: a whole 2x2x4 slice. The times are simulated.
32 devices in a mesh: group: 2 (over x), dof: 16 (over z, y, core).
Axes of the slice: x: 2, y: 2, z: 4, core: 2. Of those that a mesh axis runs over, the one named last changes fastest.
Arguments:
- panel: bfloat16 [40960, 2048], P(('group', 'dof')), parts along dimension 0, as said below
- omega: bfloat16 [2048, 256], replicated, may hold values from -0.125 to 0.125
- psi: bfloat16 [256, 20480], P(None, 'dof'), may hold values from -0.0625 to 0.0625
- phi: bfloat16 [512, 20480], P(None, 'dof'), may hold values from -0.0390625 to 0.0390625
- theta: bfloat16 [512, 2048], replicated, may hold values from -0.125 to 0.125
Outputs:
- range_sketch: float32 [40960, 256], P(('group', 'dof')), parts along dimension 0
- corange_t: float32 [4096, 256], P(('group', 'dof')), parts along dimension 0
- core_sketch: float32 [1024, 512], P('group'), parts along dimension 0
There are 2 independent parts, one for each index of `group`. A program takes and returns all parts, laid end to end along the dimension named above; an argument that names none is the same for every part. Nothing has to cross between parts.
Inputs may be any that keep to these rules, and one draw needn't show every extreme that they name: `panel`: real-valued record of order one.
All inputs are finite; a program needn't handle non-finite values.
Results may differ from a plain program's by a relative error of at most 0.0029.
Values sent between devices are 32-bit elements; how exact they have to be, the bound alone decides.
A program may use at most 64 MiB of HBM per device.

v0:
```python
import jax
import jax.numpy as jnp
from jax import lax
from jax.sharding import PartitionSpec as P


def body(panel, omega, psi, phi, theta):
    range_sketch = jnp.dot(panel, omega, preferred_element_type=jnp.float32)
    devices = lax.axis_size("dof")
    own_rows = panel.shape[1] // devices
    partial_sum = lax.dot_general(
        panel, psi, (((0,), (1,)), ((), ())), preferred_element_type=jnp.float32
    )
    summed = lax.psum(partial_sum, "dof")
    corange_t = lax.dynamic_slice_in_dim(summed, lax.axis_index("dof") * own_rows, own_rows, 0)
    right = lax.dot_general(
        panel, theta, (((1,), (1,)), ((), ())), preferred_element_type=jnp.float32
    ).astype(jnp.bfloat16)
    core_part = jnp.dot(phi, right, preferred_element_type=jnp.float32)
    core_sketch = lax.psum(core_part, "dof")
    return (range_sketch, corange_t, core_sketch)


def solution(mesh):
    in_specs = (P(("group", "dof"), None), P(), P(None, "dof"), P(None, "dof"), P())
    out_specs = (P(("group", "dof"), None), P(("group", "dof"), None), P("group", None))
    return jax.shard_map(body, mesh=mesh, in_specs=in_specs, out_specs=out_specs, check_vma=False)
```

profile of v0, /device:TPU:0, one launch (start us, length us, event | category | flops | bytes accessed | tf_op | source)
XLA Modules:
  0.0 137.5 jit_solution(393513967998479628)
XLA Ops:
  7.2 0.0 copy-start
  7.2 0.0 copy-start.1
  7.2 0.0 all-reduce.3.cloned.1.call-start
  7.2 5.7 %fusion.1 = f32[2048,256]{1,0:T(8,128)} fusion(bf16[1280,2048]{1,0:T(8,128)(2,1)} %param.5, bf16[256,1280]{1,0:T(8,128)(2,1)} %param.7), kind=kOutput, calls=%fused_computation.4 | convolution fusion | flops 1342177280 | bytes 7995392 | tf_op jit(solution)/shard_map/dot_general | solution.py:11
  12.9 0.0 copy-done
  12.9 0.0 copy-done.1
  12.9 7.1 %convolution_bitcast_fusion = f32[512,512]{0,1:T(8,128)} fusion(bf16[512,1280]{1,0:T(8,128)(2,1)S(1)} %copy-done.1, bf16[1280,2048]{1,0:T(8,128)(2,1)} %param.5, bf16[512,2048]{1,0:T(8,128)(2,1)S(1)} %copy-done), kind=kOutput, calls=%fused_computation.1 | convolution fusion | flops 3356098560 | bytes 9699328 | tf_op jit(solution)/shard_map/dot_general | solution.py:19
  20.0 0.0 copy-start.2
  20.0 0.0 all-reduce.3.cloned.1.call-update
  20.0 1.2 copy-done.2
  21.2 5.1 %fusion = f32[1280,256]{1,0:T(8,128)} fusion(bf16[1280,2048]{1,0:T(8,128)(2,1)} %param.5, bf16[2048,256]{1,0:T(8,128)(2,1)S(1)} %copy-done.2), kind=kOutput, calls=%fused_computation.3 | convolution fusion | flops 1342177280 | bytes 7602176 | tf_op jit(solution)/shard_map/dot_general | solution.py:8
  26.3 100.3 %all-reduce.3.cloned.1.call-done = (f32[2048,256]{1,0:T(8,128)}, f32[512,512]{0,1:T(8,128)}) async-done(((f32[2048,256]{1,0:T(8,128)}, f32[512,512]{0,1:T(8,128)}), (f32[2048,256]{1,0:T(8,128)}, f32[512,512]{0,1:T(8,128)})) %all-reduce.3.cloned.1.call-update) | async-done | bytes 3145744 | tf_op jit(solution)/shard_map/psum | solution.py:14
  126.6 2.5 %copy.8 = f32[512,512]{1,0:T(8,128)} copy(f32[512,512]{0,1:T(8,128)} %get-tuple-element.7) | data formatting | bytes 2097152
  129.1 1.6 %constant_dynamic-slice_fusion = f32[128,256]{1,0:T(8,128)} fusion(f32[2048,256]{1,0:T(8,128)} %get-tuple-element.6, s32[]{:T(128)S(6)} %select_n.3), kind=kLoop, calls=%fused_computation.2 | loop fusion | bytes 262148 | tf_op jit(solution)/shard_map/dynamic_slice | solution.py:15
Async XLA Ops:
  7.2 5.8 %copy-start = (bf16[512,2048]{1,0:T(8,128)(2,1)S(1)}, bf16[512,2048]{1,0:T(8,128)(2,1)}, u32[]{:S(2)}) copy-start(bf16[512,2048]{1,0:T(8,128)(2,1)} %param.9) | copy-start | bytes 6291460
  7.2 5.8 %copy-start.1 = (bf16[512,1280]{1,0:T(8,128)(2,1)S(1)}, bf16[512,1280]{1,0:T(8,128)(2,1)}, u32[]{:S(2)}) copy-start(bf16[512,1280]{1,0:T(8,128)(2,1)} %param.8) | copy-start | bytes 3932164
  7.2 119.4 %all-reduce.3.cloned.1.call-start = ((), (), s32[]{:S(2)}) async-start(), calls=%async_computation | async-start | bytes 6291456 | tf_op jit(solution)/shard_map/psum | solution.py:14
  20.0 1.2 copy-start.2
Sparse Core Ops, SparseCore 0:
  20.1 106.3 all-reduce.2
where the time goes:
time: 138 us
  waiting for transfers between devices  100 us (72%)
  matrix products  17.8 us (13%)
  between operations  14.1 us (10%)
  local copies, waits for them, and re-layouts  5.31 us (4%)
    psum x1, waiting for transfers between devices, body(): summed = lax.psum(partial_sum, 'dof')  100 us
    dot_general x1, matrix products, body(): core_part = jnp.dot(phi, right, preferred_element_type=jnp.float32)  7.05 us
    dot_general x1, matrix products, body(): lax.dot_general(panel, psi, (((0,), (1,)), ((), ())), preferred_element_t...  5.7 us
    dot_general x1, matrix products, body(): range_sketch = jnp.dot(panel, omega, preferred_element_type=jnp.float32)  5.07 us
    unnamed x7, local copies, waits for them, and re-layouts  3.74 us
  transfers between devices with their start and end apart: 1, of which 1 were waited for; matrix products, arithmetic and copies ran while one was open for 4% of the time, Pallas kernels for 0%

commit v1 on v0

v1 whole, which is shorter than its diff:
```python
import functools

import jax
import jax.numpy as jnp
from jax import lax
from jax.experimental import pallas as pl
from jax.experimental.pallas import tpu as pltpu
from jax.sharding import PartitionSpec as P

F32 = jnp.float32
LANES = 128
COLS = 256


class Exchange:
    def __init__(self, me, order, buf, recv, send_sem, recv_sem, full=None):
        self.me, self.order, self.full = me, order, full
        self.buf, self.recv = buf, recv
        self.send_sem, self.recv_sem = send_sem, recv_sem
        self.rows = buf.shape[0]
        self.stages = len(order)
        self.offs = [0]
        for stage, bit in enumerate(order):
            mine = (me // (1 << bit)) % 2
            self.offs.append(self.offs[-1] + mine * (self.rows >> (stage + 1)))
        self.copies = []
        self.done = 0

    def partner(self, bit):
        mine = (self.me // (1 << bit)) % 2
        return self.me + (1 - 2 * mine) * (1 << bit)

    def _rows(self, off, size):
        return pl.ds(pl.multiple_of(off, 8), size)

    def _start(self, src, dst, bit):
        at = len(self.copies)
        copy = pltpu.make_async_remote_copy(
            src_ref=src, dst_ref=dst, send_sem=self.send_sem.at[at], recv_sem=self.recv_sem.at[at],
            device_id={"dof": self.partner(bit)}, device_id_type=pl.DeviceIdType.MESH)
        copy.start()
        self.copies.append(copy)

    def send(self):
        stage = len(self.copies)
        half = self.rows >> (stage + 1)
        if stage < self.stages:
            bit = self.order[stage]
            mine = (self.me // (1 << bit)) % 2
            src = self.buf.at[self._rows(self.offs[stage] + (1 - mine) * half, half)]
            dst = self.recv.at[pl.ds(self.rows - (self.rows >> stage), half)]
        else:
            stage = 2 * self.stages - 1 - stage
            bit = self.order[stage]
            size = self.rows >> (stage + 1)
            src = dst = self.full.at[self._rows(self.offs[stage + 1], size)]
        self._start(src, dst, bit)

    def advance(self):
        stage = self.done
        self.copies[stage].wait_recv()
        self.done += 1
        if stage < self.stages:
            half = self.rows >> (stage + 1)
            keep = self._rows(self.offs[stage + 1], half)
            came = pl.ds(self.rows - (self.rows >> stage), half)
            last = stage == self.stages - 1
            out = self.full if last and self.full is not None else self.buf
            out[keep] = self.buf[keep] + self.recv[came]
        if not self.finished():
            self.send()

    def finished(self):
        return self.done == self.stages * (2 if self.full is not None else 1)

    def drain(self):
        for copy in self.copies:
            copy.wait_send()


def position(device, order):
    at = 0
    for bit in order:
        at = 2 * at + (device >> bit) % 2
    return at


def kernel(n, orders_r, orders_c, panel_h, omega_h, psi_h, phi_h, theta_h, range_h, corange_h, core_h,
           panel, omega, psi, phi, theta, right, rng, rbuf, rrecv, cbuf, crecv, cfull,
           load_sem, out_sem, rsend, rrecv_sem, csend, crecv_sem):
    me = lax.axis_index("dof")
    bits = n.bit_length() - 1
    dof, snaps = panel.shape
    blocks = snaps // COLS
    nr, nc = len(orders_r), len(orders_c)
    own = snaps // n
    sub = own // nr
    core = phi.shape[0]

    loads = [pltpu.make_async_copy(psi_h, psi, load_sem.at[0])]
    for j in range(blocks):
        loads.append(pltpu.make_async_copy(
            panel_h.at[:, pl.ds(j * COLS, COLS)], panel.at[:, pl.ds(j * COLS, COLS)], load_sem.at[1 + j]))
    loads.append(pltpu.make_async_copy(theta_h, theta, load_sem.at[1 + blocks]))
    loads.append(pltpu.make_async_copy(phi_h, phi, load_sem.at[2 + blocks]))
    loads.append(pltpu.make_async_copy(omega_h, omega, load_sem.at[3 + blocks]))
    for load in loads:
        load.start()

    barrier = pltpu.get_barrier_semaphore()
    for bit in range(bits):
        mine = (me // (1 << bit)) % 2
        pl.semaphore_signal(barrier, inc=1, device_id={"dof": me + (1 - 2 * mine) * (1 << bit)},
                            device_id_type=pl.DeviceIdType.MESH)

    loads[0].wait()
    for j in range(blocks):
        loads[1 + j].wait()
        block = jnp.dot(psi[...], panel[:, j * COLS:(j + 1) * COLS], preferred_element_type=F32).T
        for k in range(COLS // sub):
            row = j * COLS + k * sub
            device, chunk = row // own, (row % own) // sub
            at = position(device, orders_r[chunk]) * sub
            rbuf[chunk, at:at + sub, :] = block[k * sub:(k + 1) * sub, :]

    pl.semaphore_wait(barrier, bits)
    xr = [Exchange(me, order, rbuf.at[c], rrecv.at[c], rsend.at[c], rrecv_sem.at[c])
          for c, order in enumerate(orders_r)]
    xc = [Exchange(me, order, cbuf.at[c], crecv.at[c], csend.at[c], crecv_sem.at[c], cfull.at[c])
          for c, order in enumerate(orders_c)]
    for x in xr:
        x.send()

    loads[1 + blocks].wait()
    tile = 256

    def right_tile(i, _):
        rows = pl.ds(pl.multiple_of(i * tile, tile), tile)
        right[rows, :] = lax.dot_general(
            panel[rows, :], theta[...], (((1,), (1,)), ((), ())), preferred_element_type=F32).astype(right.dtype)
        return _

    tiles = dof // tile
    lax.fori_loop(0, tiles // 2, right_tile, 0)
    xr[0].advance()
    xr[-1].advance()
    lax.fori_loop(tiles // 2, tiles, right_tile, 0)

    loads[2 + blocks].wait()
    per = core // LANES // nc
    for c in range(nc):
        part = jnp.dot(phi[...], right[:, c * per * LANES:(c + 1) * per * LANES], preferred_element_type=F32)
        for g in range(per):
            cbuf[c, g * core:(g + 1) * core, :] = part[:, g * LANES:(g + 1) * LANES]
        xc[c].send()
    for x in xr[1:-1]:
        x.advance()
    for x in xc:
        x.advance()

    loads[3 + blocks].wait()

    def range_tile(i, _):
        rows = pl.ds(pl.multiple_of(i * tile, tile), tile)
        rng[rows, :] = jnp.dot(panel[rows, :], omega[...], preferred_element_type=F32)
        return _

    lax.fori_loop(0, tiles, range_tile, 0)
    outs = [pltpu.make_async_copy(rng, range_h, out_sem.at[0])]
    outs[0].start()

    def finish_r(c):
        x = xr[c]
        copy = pltpu.make_async_copy(
            x.buf.at[x._rows(x.offs[-1], sub)], corange_h.at[pl.ds(c * sub, sub)], out_sem.at[1 + c])
        copy.start()
        outs.append(copy)

    def finish_c(c):
        for g in range(per):
            copy = pltpu.make_async_copy(
                xc[c].full.at[pl.ds(g * core, core)], core_h.at[:, pl.ds((c * per + g) * LANES, LANES)],
                out_sem.at[1 + nr + c * per + g])
            copy.start()
            outs.append(copy)

    while not all(x.finished() for x in xr + xc):
        for c, x in enumerate(xc):
            if not x.finished():
                x.advance()
                if x.finished():
                    finish_c(c)
        for c, x in enumerate(xr):
            if not x.finished():
                x.advance()
                if x.finished():
                    finish_r(c)
    for x in xr + xc:
        x.drain()
    for copy in outs:
        copy.wait()


def body(n, panel, omega, psi, phi, theta):
    dof, snaps = panel.shape
    rank, corange, core = omega.shape[1], psi.shape[0], phi.shape[0]
    bits = n.bit_length() - 1
    order_a = tuple(range(bits))
    order_b = (0, 2, 1) + tuple(range(3, bits)) if bits > 2 else order_a
    nr = min(4, snaps // n // 8)
    nc = min(4, core * core // LANES // n // 8)
    orders_r = (order_a,) * (nr - 1) + (order_b,)
    orders_c = (order_a,) * (nc - 1) + (order_b,)
    rrows, crows = snaps // nr, core * core // LANES // nc
    blocks = snaps // COLS
    any_space = pl.BlockSpec(memory_space=pl.ANY)
    dma = pltpu.SemaphoreType.DMA
    return pl.pallas_call(
        functools.partial(kernel, n, orders_r, orders_c),
        out_shape=(
            jax.ShapeDtypeStruct((dof, rank), F32),
            jax.ShapeDtypeStruct((snaps // n, corange), F32),
            jax.ShapeDtypeStruct((core, core), F32),
        ),
        in_specs=[any_space] * 5,
        out_specs=(any_space,) * 3,
        scratch_shapes=[
            pltpu.VMEM(panel.shape, panel.dtype),
            pltpu.VMEM(omega.shape, omega.dtype),
            pltpu.VMEM(psi.shape, psi.dtype),
            pltpu.VMEM(phi.shape, phi.dtype),
            pltpu.VMEM(theta.shape, theta.dtype),
            pltpu.VMEM((dof, core), jnp.bfloat16),
            pltpu.VMEM((dof, rank), F32),
            pltpu.VMEM((nr, rrows, corange), F32),
            pltpu.VMEM((nr, rrows, corange), F32),
            pltpu.VMEM((nc, crows, LANES), F32),
            pltpu.VMEM((nc, crows, LANES), F32),
            pltpu.VMEM((nc, crows, LANES), F32),
            dma((4 + blocks,)),
            dma((1 + nr + core // LANES,)),
            dma((nr, bits)),
            dma((nr, bits)),
            dma((nc, 2 * bits)),
            dma((nc, 2 * bits)),
        ],
        compiler_params=pltpu.CompilerParams(
            collective_id=0, has_side_effects=True, vmem_limit_bytes=40 * 1024 * 1024),
        cost_estimate=pl.CostEstimate(
            flops=2 * dof * snaps * (rank + corange + core) + 2 * dof * core * core,
            bytes_accessed=2 * dof * snaps * 2, transcendentals=0),
        name="sketches",
    )(panel, omega, psi, phi, theta)


def solution(mesh):
    in_specs = (P(("group", "dof"), None), P(), P(None, "dof"), P(None, "dof"), P())
    out_specs = (P(("group", "dof"), None), P(("group", "dof"), None), P("group", None))
    return jax.shard_map(functools.partial(body, mesh.shape["dof"]), mesh=mesh, in_specs=in_specs,
                         out_specs=out_specs, check_vma=False)
```

time: 138 us -> 66.5 us (0.48)
  waiting for transfers between devices: 100 us -> 0 us
  Pallas kernels: 0 us -> 55.1 us
  matrix products: 17.8 us -> 0 us
  between operations: 14.1 us -> 0.65 us
  local copies, waits for them, and re-layouts: 5.31 us -> 10.4 us
    psum x1 -> x0, waiting for transfers between devices: 100 us -> none  [body(): summed = lax.psum(partial_sum, 'dof')]
    pallas_call x0 -> x1, Pallas kernels: none -> 55.1 us  [body(): pl.pallas_call(functools.partial(kernel, n, orders_r, orders_c), out_shap...]
    dot_general x3 -> x0, matrix products: 17.8 us -> none  [the longest x1 7.05 us: body(): core_part = jnp.dot(phi, right, preferred_element_type=jnp.float32)]
    unnamed x7 -> x13, local copies, waits for them, and re-layouts: 3.74 us -> 10.4 us
    dynamic_slice x1 -> x0, local copies, waits for them, and re-layouts: 1.57 us -> none  [body(): lax.dynamic_slice_in_dim(summed, lax.axis_index('dof') * own_rows, own_ro...]
  transfers between devices with their start and end apart: 1 -> 0, of which waited for: 1 -> 0; matrix products, arithmetic and copies ran while one was open for 4% -> 0% of each run, Pallas kernels for 0% -> 0%
where the time goes in v1:
time: 66.5 us; the launch traced here: 66.2 us
  Pallas kernels  55.1 us (83%)
  local copies, waits for them, and re-layouts  10.4 us (16%)
    pallas_call x1, Pallas kernels, body(): pl.pallas_call(functools.partial(kernel, n, orders_r, orders_c), out_shap...  55.1 us
    unnamed x13, local copies, waits for them, and re-layouts  10.4 us

profile of v1, /device:TPU:0, one launch (start us, length us, event | category | flops | bytes accessed | tf_op | source)
XLA Modules:
  0.0 66.2 jit_solution(12342603469209314537)
XLA Ops:
  0.6 0.0 copy-start
  0.6 2.5 %copy-done = bf16[1280,2048]{1,0:T(8,128)(2,1)S(1)} copy-done((bf16[1280,2048]{1,0:T(8,128)(2,1)S(1)}, bf16[1280,2048]{1,0:T(8,128)(2,1)}, u32[]{:S(2)}) %copy-start) | copy-done | bytes 5242904
  3.1 0.0 copy-start.1
  3.1 1.6 %copy-done.1 = bf16[512,2048]{1,0:T(8,128)(2,1)S(1)} copy-done((bf16[512,2048]{1,0:T(8,128)(2,1)S(1)}, bf16[512,2048]{1,0:T(8,128)(2,1)}, u32[]{:S(2)}) %copy-start.1) | copy-done | bytes 2097176
  4.7 0.0 copy-start.2
  4.7 1.3 %copy-done.2 = bf16[512,1280]{1,0:T(8,128)(2,1)S(1)} copy-done((bf16[512,1280]{1,0:T(8,128)(2,1)S(1)}, bf16[512,1280]{1,0:T(8,128)(2,1)}, u32[]{:S(2)}) %copy-start.2) | copy-done | bytes 1310744
  6.0 0.0 copy-start.3
  6.0 1.2 %copy-done.3 = bf16[2048,256]{1,0:T(8,128)(2,1)S(1)} copy-done((bf16[2048,256]{1,0:T(8,128)(2,1)S(1)}, bf16[2048,256]{1,0:T(8,128)(2,1)}, u32[]{:S(2)}) %copy-start.3) | copy-done | bytes 1048600
  7.3 0.0 copy-start.4
  7.3 1.1 %copy-done.4 = bf16[256,1280]{1,0:T(8,128)(2,1)S(1)} copy-done((bf16[256,1280]{1,0:T(8,128)(2,1)S(1)}, bf16[256,1280]{1,0:T(8,128)(2,1)}, u32[]{:S(2)}) %copy-start.4) | copy-done | bytes 655384
  8.3 55.1 %sketches.1 = (f32[1280,256]{1,0:T(8,128)S(1)}, f32[128,256]{1,0:T(8,128)S(1)}, f32[512,512]{1,0:T(8,128)S(1)}) custom-call(bf16[1280,2048]{1,0:T(8,128)(2,1)S(1)} %copy-done, bf16[2048,256]{1,0:T(8,128)(2,1)S(1)} %copy-done.3, bf16[256,1280]{1,0:T(8,128)(2,1)S(1)} %copy-done.4, bf16[512,1280]{1,0:T(8,128)(2,1)S(1)} %copy-done.2, bf16[512,2048]{1,0:T(8,128)(2,1)S(1)} %copy-done.1), custom_call_target="tpu_custom_call" | custom-call | flops 6039797760 | bytes 10485760 | tf_op jit(solution)/shard_map/sketches/pallas_call | solution.py:218
  63.5 1.1 %copy.11 = f32[1280,256]{1,0:T(8,128)} copy(f32[1280,256]{1,0:T(8,128)S(1)} %get-tuple-element.6) | data formatting | bytes 2621440
  64.5 0.7 copy.12
  65.2 1.0 %copy.13 = f32[512,512]{1,0:T(8,128)} copy(f32[512,512]{1,0:T(8,128)S(1)} %get-tuple-element.8) | data formatting | bytes 2097152
Async XLA Ops:
  0.6 2.5 %copy-start = (bf16[1280,2048]{1,0:T(8,128)(2,1)S(1)}, bf16[1280,2048]{1,0:T(8,128)(2,1)}, u32[]{:S(2)}) copy-start(bf16[1280,2048]{1,0:T(8,128)(2,1)} %panel_h.1) | copy-start | bytes 15728644
  3.1 1.6 %copy-start.1 = (bf16[512,2048]{1,0:T(8,128)(2,1)S(1)}, bf16[512,2048]{1,0:T(8,128)(2,1)}, u32[]{:S(2)}) copy-start(bf16[512,2048]{1,0:T(8,128)(2,1)} %theta_h.1) | copy-start | bytes 6291460
  4.7 1.3 %copy-start.2 = (bf16[512,1280]{1,0:T(8,128)(2,1)S(1)}, bf16[512,1280]{1,0:T(8,128)(2,1)}, u32[]{:S(2)}) copy-start(bf16[512,1280]{1,0:T(8,128)(2,1)} %phi_h.1) | copy-start | bytes 3932164
  6.0 1.2 %copy-start.3 = (bf16[2048,256]{1,0:T(8,128)(2,1)S(1)}, bf16[2048,256]{1,0:T(8,128)(2,1)}, u32[]{:S(2)}) copy-start(bf16[2048,256]{1,0:T(8,128)(2,1)} %omega_h.1) | copy-start | bytes 3145732
  7.3 1.1 %copy-start.4 = (bf16[256,1280]{1,0:T(8,128)(2,1)S(1)}, bf16[256,1280]{1,0:T(8,128)(2,1)}, u32[]{:S(2)}) copy-start(bf16[256,1280]{1,0:T(8,128)(2,1)} %psi_h.1) | copy-start | bytes 1966084
